TPU v7x, 256 devices: a whole 4x4x8 slice. The times are simulated.
256 devices in a mesh: layer: 4 (over y), perm: 8 (over z), owner: 8 (over x, core).
Axes of the slice: x: 4, y: 4, z: 8, core: 2. Of those that a mesh axis runs over, the one named last changes fastest.
Arguments:
- amplitudes: bfloat16 [1024, 32768], P(('layer', 'perm'), 'owner'), may hold values from -6 to 6
- integrals: bfloat16 [32768, 16384], P(('layer', 'perm'), 'owner'), may hold values from -0.125 to 0.125
- contract_irrep: int32 [256], replicated, may hold values from 0 to 3
- output_irrep: int32 [128], replicated, may hold values from 0 to 3
- occ_energy: float32 [1024], P(('layer', 'perm')), may hold values from -4 to -0.5
- virt_energy: float32 [16384], P('owner'), may hold values from 0.5 to 4
Outputs:
- ladder_update: float32 [1024, 16384], P(('layer', 'perm'), 'owner')
All inputs are finite; a program needn't handle non-finite values.
Results may differ from a plain program's by a relative error of at most 0.0003.
Values may be sent and summed in bfloat16 or wider, within the bound.
A program may use at most 64 MiB of HBM per device.

v0:
```python
import jax
import jax.numpy as jnp
from jax import lax
from jax.sharding import PartitionSpec as P

BW = 128


def local(amplitudes, integrals, contract_irrep, output_irrep, occ_energy, virt_energy):
    gathered = lax.all_gather(amplitudes, "owner", axis=1, tiled=True)
    ordered = lax.all_to_all(gathered, ("layer", "perm"), split_axis=1, concat_axis=0, tiled=True)
    inner_width = integrals.shape[0]
    outer_width = integrals.shape[1]
    inner_blocks = inner_width // BW
    outer_blocks = outer_width // BW
    inner_offset = lax.axis_index(("layer", "perm")) * inner_blocks
    outer_offset = lax.axis_index("owner") * outer_blocks
    row_irrep = jnp.repeat(
        lax.dynamic_slice_in_dim(contract_irrep, inner_offset, inner_blocks, 0),
        BW,
        total_repeat_length=inner_width,
    )
    column_irrep = jnp.repeat(
        lax.dynamic_slice_in_dim(output_irrep, outer_offset, outer_blocks, 0),
        BW,
        total_repeat_length=outer_width,
    )
    matching = row_irrep[:, None] == column_irrep[None, :]
    sector = jnp.where(matching, integrals, jnp.zeros_like(integrals))
    ladder = lax.psum_scatter(
        jnp.dot(ordered, sector, preferred_element_type=jnp.float32),
        ("layer", "perm"),
        scatter_dimension=0,
        tiled=True,
    )
    return ladder / (virt_energy[None, :] - occ_energy[:, None])


def solution(mesh):
    return jax.shard_map(
        local,
        mesh=mesh,
        in_specs=(
            P(("layer", "perm"), "owner"),
            P(("layer", "perm"), "owner"),
            P(),
            P(),
            P(("layer", "perm")),
            P("owner"),
        ),
        out_specs=P(("layer", "perm"), "owner"),
        check_vma=False,
    )
```

profile of v0, /device:TPU:8, one launch (start us, length us, event | category | flops | bytes accessed | tf_op | source)
XLA Modules:
  0.0 355.7 jit_solution(869948714398403630)
XLA Ops:
  6.5 0.0 all-gather.2.cloned.1.call-start
  6.5 0.7 all-gather.2.cloned.1.call-update
  7.3 32.5 %all-gather.2.cloned.1.call-done = bf16[32,32768]{1,0:T(8,128)(2,1)} async-done(((bf16[32,4096]{1,0:T(8,128)(2,1)}), bf16[32,32768]{1,0:T(8,128)(2,1)}) %all-gather.2.cloned.1.call-update) | async-done | bytes 2097168 | tf_op jit(solution)/shard_map/all_gather | solution.py:10
  39.8 3.2 copy.19
  43.0 10.2 %all-to-all-start = ((bf16[32,32,1024]{2,0,1:T(8,128)(2,1)}), bf16[32,32,1024]{2,0,1:T(8,128)(2,1)S(1)}, u32[]{:S(2)}, u32[]{:S(2)}) async-start(bf16[32,32,1024]{2,0,1:T(8,128)(2,1)} %bitcast.56), calls=%async_computation | async-start | bytes 4194304 | tf_op jit(solution)/shard_map/all_to_all | solution.py:11
  53.2 0.0 reduce-scatter.4.cloned.1.call-start
  53.2 0.0 copy-done.3
  53.3 0.1 dynamic_slice.7
  53.3 0.0 copy-done.2
  53.3 0.1 dynamic_slice.6
  53.4 0.7 fusion.8
  54.1 0.7 fusion.9
  54.8 4.3 %compare_select_fusion.3 = (s32[2048,1]{0,1:T(1,128)S(1)}, s32[2048,1]{0,1:T(1,128)S(1)}) fusion(s32[]{:T(128)} %bitcast.26, s32[]{:T(128)} %bitcast.27, s32[]{:T(128)} %bitcast.28, s32[]{:T(128)} %bitcast.29, s32[]{:T(128)} %bitcast.30, s32[]{:T(128)} %bitcast.32, s32[]{:T(128)} %bitcast.31, s32[2048,1]{0,1:T(1,128)S(1)} %bitcast.65, s32[2048,1]{0,1:T(1,128)S(1)} %bitcast.64), kind=kLoop, calls=%fused_computation.17 | loop fusion | flops 28672 | bytes 32796 | tf_op jit(solution)/shard_map/jit(_take)/gather | solution.py:23
  59.2 0.2 compare_reduce_fusion.8
  59.4 4.3 %compare_select_fusion.11 = s32[1024,1]{0,1:T(1,128)S(1)} fusion(s32[]{:T(128)} %bitcast.5, s32[]{:T(128)} %bitcast.6, s32[]{:T(128)} %bitcast.7, s32[]{:T(128)} %bitcast.8, s32[]{:T(128)} %bitcast.9, s32[]{:T(128)} %bitcast.11, s32[]{:T(128)} %bitcast.10, s32[1024,1]{0,1:T(1,128)S(1)} %bitcast.62, s32[1024,1]{0,1:T(1,128)S(1)} %bitcast.60), kind=kLoop, calls=%fused_computation.26 | loop fusion | flops 14336 | bytes 12316 | tf_op jit(solution)/shard_map/jit(_take)/gather | solution.py:18
  63.6 0.6 select_select_fusion.1
  64.3 5.7 %select_select_fusion = s32[2048]{0:T(1024)S(1)} fusion(pred[2048]{0:T(1024)(128)(4,1)S(1)} %get-tuple-element.37, pred[2048]{0:T(1024)(128)(4,1)S(1)} %get-tuple-element.36, pred[2048]{0:T(1024)(128)(4,1)S(1)} %get-tuple-element.35, pred[2048]{0:T(1024)(128)(4,1)S(1)} %get-tuple-element.34, pred[2048]{0:T(1024)(128)(4,1)S(1)} %get-tuple-element.33, ...), kind=kLoop, calls=%fused_computation.33 | loop fusion | flops 36864 | bytes 34852 | tf_op jit(solution)/shard_map/jit(_take)/select_n | solution.py:23
  70.0 31.1 %all-to-all-done = bf16[32,32,1024]{2,0,1:T(8,128)(2,1)S(1)} async-done(((bf16[32,32,1024]{2,0,1:T(8,128)(2,1)}), bf16[32,32,1024]{2,0,1:T(8,128)(2,1)S(1)}, u32[]{:S(2)}, u32[]{:S(2)}) %all-to-all-start) | async-done | bytes 2097184 | tf_op jit(solution)/shard_map/all_to_all | solution.py:11
  101.1 9.6 %convolution_bitcast_fusion = f32[1024,2048]{0,1:T(8,128)} fusion(bf16[1024,1024]{1,0:T(8,128)(2,1)S(1)} %bitcast.57, bf16[1024,2048]{1,0:T(8,128)(2,1)} %param.11, s32[2048]{0:T(1024)S(1)} %select_select_fusion, s32[1024]{0:T(1024)S(1)} %select_select_fusion.1), kind=kOutput, calls=%fused_computation.1 | convolution fusion | flops 4299161600 | bytes 14692352 | tf_op jit(solution)/shard_map/dot_general | solution.py:31
  110.7 9.1 %copy.15 = f32[1024,2048]{1,0:T(8,128)} copy(f32[1024,2048]{0,1:T(8,128)} %convolution_bitcast_fusion) | data formatting | bytes 16777216
  119.9 0.0 reduce-scatter.4.cloned.1.call-update
  119.9 227.2 %reduce-scatter.4.cloned.1.call-done = f32[32,2048]{1,0:T(8,128)} async-done(((f32[1024,2048]{1,0:T(8,128)}), f32[32,2048]{1,0:T(8,128)}) %reduce-scatter.4.cloned.1.call-update) | async-done | bytes 262160 | tf_op jit(solution)/shard_map/reduce_scatter | solution.py:30
  347.1 0.0 copy-done
  347.1 1.8 subtract_divide_fusion
  (10 shorter events, 0.1 us)
Async XLA Ops:
  6.5 33.3 %all-gather.2.cloned.1.call-start = ((), (), s32[]{:S(2)}) async-start(), calls=%async_computation.2 | async-start | bytes 2359296 | tf_op jit(solution)/shard_map/all_gather | solution.py:10
  39.8 13.4 %copy-start.3 = (s32[128]{0:T(128)S(1)}, s32[128]{0:T(128)}, u32[]{:S(2)}) copy-start(s32[128]{0:T(128)} %param.13) | copy-start | bytes 1540
  39.8 13.5 %copy-start.2 = (s32[256]{0:T(256)S(1)}, s32[256]{0:T(256)}, u32[]{:S(2)}) copy-start(s32[256]{0:T(256)} %param.12) | copy-start | bytes 3076
  43.0 58.1 %all-to-all-start = ((bf16[32,32,1024]{2,0,1:T(8,128)(2,1)}), bf16[32,32,1024]{2,0,1:T(8,128)(2,1)S(1)}, u32[]{:S(2)}, u32[]{:S(2)}) async-start(bf16[32,32,1024]{2,0,1:T(8,128)(2,1)} %bitcast.56), calls=%async_computation | async-start | bytes 4194304 | tf_op jit(solution)/shard_map/all_to_all | solution.py:11
  53.2 293.9 %reduce-scatter.4.cloned.1.call-start = ((), (), s32[]{:S(2)}) async-start(), calls=%async_computation.3 | async-start | bytes 8650752 | tf_op jit(solution)/shard_map/reduce_scatter | solution.py:30
  119.9 227.2 %copy-start = (f32[2048]{0:T(1024)S(1)}, f32[2048]{0:T(1024)}, u32[]{:S(2)}) copy-start(f32[2048]{0:T(1024)} %param.15) | copy-start | bytes 24580
  119.9 227.2 %copy-start.1 = (f32[32]{0:T(128)S(1)}, f32[32]{0:T(128)}, u32[]{:S(2)}) copy-start(f32[32]{0:T(128)} %param.14) | copy-start | bytes 388
Sparse Core Ops, SparseCore 0:
  9.2 30.5 all-gather.1
  120.0 227.0 reduce-scatter.3
where the time goes:
time: 357 us; the launch traced here: 356 us
  waiting for transfers between devices  292 us (82%)
  other arithmetic  16.9 us (5%)
  local copies, waits for them, and re-layouts  13.9 us (4%)
  between operations  13.5 us (4%)
  starting transfers between devices  10.2 us (3%)
  matrix products  9.64 us (3%)
    reduce_scatter x1, waiting for transfers between devices, local(): lax.psum_scatter(jnp.dot(ordered, sector, preferred_element_type=jnp.floa...  227 us
    all_gather x1, waiting for transfers between devices, local(): gathered = lax.all_gather(amplitudes, 'owner', axis=1, tiled=True)  32.5 us
    all_to_all x1, waiting for transfers between devices, local(): lax.all_to_all(gathered, ('layer', 'perm'), split_axis=1, concat_axis=0,...  31.1 us
    all_to_all x1, starting transfers between devices, local(): lax.all_to_all(gathered, ('layer', 'perm'), split_axis=1, concat_axis=0,...  10.2 us
    dot_general x1, matrix products, local(): jnp.dot(ordered, sector, preferred_element_type=jnp.float32)  9.64 us
    unnamed x9, local copies, waits for them, and re-layouts  9.15 us
  transfers between devices with their start and end apart: 3, of which 3 were waited for; matrix products, arithmetic and copies ran while one was open for 5% of the time, Pallas kernels for 0%

commit v1 on v0

v1 whole, which is shorter than its diff:
```python
import functools

import jax
import jax.numpy as jnp
from jax import lax
from jax.experimental import pallas as pl
from jax.experimental.pallas import tpu as pltpu
from jax.sharding import PartitionSpec as P

BW = 128
LANES = 128
CHUNK = 32
PIECE = 256
NY = 5
TOP = 32767.0
MESH = pl.DeviceIdType.MESH


class Ring:
    def __init__(self, axis, n, groups, own, bufs):
        self.axis, self.n, self.groups, self.own = axis, n, groups, own
        self.sq, self.rq, self.ss, self.rs, self.sems = bufs
        self.me = lax.axis_index(axis)

    def copies(self, p, t, d):
        where = {self.axis: lax.rem(self.me + (1 if d == 0 else self.n - 1), self.n)}
        at = (p, t, d, d) if t == 0 else (p, t, d)
        return [
            pltpu.make_async_remote_copy(
                src_ref=self.sq.at[at],
                dst_ref=self.rq.at[at],
                send_sem=self.sems.at[0, p, t, d],
                recv_sem=self.sems.at[1, p, t, d],
                device_id=where,
                device_id_type=MESH,
            ),
            pltpu.make_async_remote_copy(
                src_ref=self.ss.at[p, t, d],
                dst_ref=self.rs.at[p, t, d],
                send_sem=self.sems.at[2, p, t, d],
                recv_sem=self.sems.at[3, p, t, d],
                device_id=where,
                device_id_type=MESH,
            ),
        ]

    def each_group(self, body):
        if self.groups == 1:
            body(0)
        else:
            def step(g, carry):
                body(g)
                return carry

            lax.fori_loop(0, self.groups, step, 0, unroll=2)

    def rows(self, g):
        return pl.ds(g * CHUNK if isinstance(g, int) else pl.multiple_of(g * CHUNK, CHUNK), CHUNK)

    def decode(self, p, t, d, h, g):
        coded = self.rq[p, t, d, h, self.rows(g), :].astype(jnp.int32).astype(jnp.float32)
        return coded * self.rs[p, t, d, pl.ds(g, 1), :]

    def wait(self, p, t, d):
        for copy in self.copies(p, t, d):
            copy.wait_recv()

    def send(self, p, t):
        half = self.n // 2
        for d in range(2):
            dest = lax.rem(self.me + (half - t if d == 0 else half + t), self.n)
            if t > 0:
                self.wait(p, t - 1, d)

            def body(g, d=d, dest=dest):
                halves = (d,) if t == 0 else (0, 1)
                values = []
                for h in halves:
                    value = self.own(p, dest, g, h)
                    if t > 1 or (t == 1 and h == d):
                        value = value + self.decode(p, t - 1, d, h, g)
                    values.append(value)
                most = jnp.max(functools.reduce(jnp.maximum, [jnp.abs(v) for v in values]), axis=0, keepdims=True)
                scale = jnp.maximum(most, 1e-30) * (1.0 / TOP)
                factor = 1.0 / scale
                self.ss[p, t, d, pl.ds(g, 1), :] = scale
                for h, value in zip(halves, values):
                    coded = jnp.round(value * factor).astype(jnp.int32).astype(jnp.int16)
                    self.sq[p, t, d, h, self.rows(g), :] = coded

            self.each_group(body)
            for copy in self.copies(p, t, d):
                copy.start()

    def final(self, p, store):
        last = self.n // 2 - 1
        for d in range(2):
            self.wait(p, last, d)

        def body(g):
            for h in range(2):
                total = self.own(p, self.me, g, h) + self.decode(p, last, 0, h, g)
                store(p, g, h, total + self.decode(p, last, 1, h, g))

        self.each_group(body)

    def drain(self, pieces):
        def step(p, carry):
            for t in range(self.n // 2):
                for d in range(2):
                    for copy in self.copies(p, t, d):
                        copy.wait_send()
            return carry

        lax.fori_loop(0, pieces, step, 0)


def kernel(ny, nz, nx, cirr, oirr, amp, integ, out, abuf, im, part, qy, qz, asems, *ring_bufs):
    y, z, o = lax.axis_index("layer"), lax.axis_index("perm"), lax.axis_index("owner")
    x, c = o // 2, lax.rem(o, 2)
    pieces = im.shape[1] // PIECE
    n_z = pieces - NY
    depth = im.shape[0]
    per_core = nz // 2
    groups = nz // 2
    s1_send, s1_recv, x_send, x_recv, y_send, y_recv, b_send, b_recv, i_sem = asems

    barrier = pltpu.get_barrier_semaphore()
    for k in range(1, nz):
        pl.semaphore_signal(barrier, inc=1, device_id={"perm": lax.rem(z + k, nz)}, device_id_type=MESH)
    for k in range(1, ny):
        pl.semaphore_signal(barrier, inc=1, device_id={"layer": lax.rem(y + k, ny)}, device_id_type=MESH)
    for k in range(1, nx):
        pl.semaphore_signal(barrier, inc=1, device_id={"owner": lax.rem(o + 2 * k, 2 * nx)}, device_id_type=MESH)
    pl.semaphore_signal(barrier, inc=1, device_id={"owner": o + 1 - 2 * c}, device_id_type=MESH)

    load = [
        pltpu.make_async_copy(integ.at[pl.ds(k * BW, BW)], im.at[pl.ds(k * BW, BW)], i_sem.at[k])
        for k in range(depth // BW)
    ]
    for copy in load:
        copy.start()
    pl.semaphore_wait(barrier, nz + ny + nx - 2)

    spare = ny * nz

    def slot(source_x, at_y, zs):
        return jnp.where(source_x == at_y, at_y * nz + zs, spare + source_x * nz + zs)

    def along_z(j):
        return pltpu.make_async_remote_copy(
            src_ref=amp.at[:, pl.ds(j * depth, depth)],
            dst_ref=abuf.at[slot(x, y, z)],
            send_sem=s1_send.at[j],
            recv_sem=s1_recv.at[z],
            device_id={"perm": c * per_core + j},
            device_id_type=MESH,
        )

    for j in range(per_core):
        @pl.when(c * per_core + j != z)
        def _(j=j):
            along_z(j).start()

        @pl.when(c * per_core + j == z)
        def _(j=j):
            pltpu.make_async_copy(amp.at[:, pl.ds(j * depth, depth)], abuf.at[slot(x, y, z)], s1_recv.at[z]).start()

    outer = im.shape[1] // BW
    inner_base = (y * nz + z) * (depth // BW)
    outer_base = o * outer
    for copy in load:
        copy.wait()

    def mask_rows(k, carry):
        row_irrep = cirr[inner_base + k]
        rows = pl.ds(pl.multiple_of(k * BW, BW), BW)
        for b in range(outer):
            cols = pl.ds(b * BW, BW)
            block = im[rows, cols]
            im[rows, cols] = jnp.where(row_irrep == oirr[outer_base + b], block, jnp.zeros_like(block))
        return carry

    lax.fori_loop(0, depth // BW, mask_rows, 0)

    active = c == z // per_core

    def pair(first):
        return abuf.at[pl.ds(first, 2)]

    def along_x(g, k):
        return pltpu.make_async_remote_copy(
            src_ref=pair(slot(x, y, 2 * g)),
            dst_ref=pair(slot(x, y, 2 * g)),
            send_sem=x_send.at[g, k],
            recv_sem=x_recv.at[g, k],
            device_id={"owner": lax.rem(o + 2 * k, 2 * nx)},
            device_id_type=MESH,
        )

    def along_y(g, k, xs):
        return pltpu.make_async_remote_copy(
            src_ref=pair(spare + xs * nz + 2 * g),
            dst_ref=pair(y * nz + 2 * g),
            send_sem=y_send.at[g, k],
            recv_sem=y_recv.at[g, y],
            device_id={"layer": xs},
            device_id_type=MESH,
        )

    def from_y(g, ys):
        return pltpu.make_async_remote_copy(
            src_ref=pair(ys * nz + 2 * g),
            dst_ref=pair(ys * nz + 2 * g),
            send_sem=y_send.at[g, 0],
            recv_sem=y_recv.at[g, ys],
            device_id={"layer": ys},
            device_id_type=MESH,
        )

    def across(g, ys):
        return pltpu.make_async_remote_copy(
            src_ref=pair(ys * nz + 2 * g),
            dst_ref=pair(ys * nz + 2 * g),
            send_sem=b_send.at[g, ys],
            recv_sem=b_recv.at[g, ys],
            device_id={"owner": o + 1 - 2 * c},
            device_id_type=MESH,
        )

    order = [0, 1, groups - 1] + list(range(2, groups - 1))
    near = [1, 3, 2]

    @pl.when(active)
    def _():
        def hand_on(g, k):
            xs = lax.rem(x + k, nx)

            @pl.when(xs != y)
            def _():
                along_y(g, k, xs).start()

            @pl.when(xs == y)
            def _():
                across(g, y).start()

        for t in order:
            g = lax.rem(z // 2 + t, groups)
            for e in range(2):
                pltpu.make_async_copy(abuf.at[slot(x, y, 2 * g + e)], abuf.at[slot(x, y, 2 * g + e)], s1_recv.at[2 * g + e]).wait()
            for k in near:
                along_x(g, k).start()
            hand_on(g, 0)
        for t in order:
            g = lax.rem(z // 2 + t, groups)
            for k in near:
                xs = lax.rem(x + k, nx)
                pltpu.make_async_copy(pair(slot(xs, y, 2 * g)), pair(slot(xs, y, 2 * g)), x_recv.at[g, nx - k]).wait()
                hand_on(g, k)
        for t in order:
            g = lax.rem(z // 2 + t, groups)
            for k in near:
                ys = lax.rem(y + k, ny)
                from_y(g, ys).wait_recv()
                across(g, ys).start()

    @pl.when(jnp.logical_not(active))
    def _():
        for t in order:
            g = lax.rem(z // 2 + t, groups)
            for ys in range(ny):
                across(g, ys).wait_recv()

    def own_part(base, y_first):
        def own(p, dest, g, h):
            row = (dest * nz + g if y_first else g * nz + dest) * CHUNK
            return part[base + p, h, pl.ds(pl.multiple_of(row, CHUNK), CHUNK), :]
        return own

    def own_sum(ref):
        return lambda p, dest, g, h: ref[p, h, pl.ds(pl.multiple_of(dest * CHUNK, CHUNK), CHUNK), :]

    bufs = [ring_bufs[5 * k: 5 * k + 5] for k in range(4)]
    y1 = Ring("layer", ny, nz, own_part(0, True), bufs[0])
    z2 = Ring("perm", nz, 1, own_sum(qy), bufs[1])
    z1 = Ring("perm", nz, ny, own_part(NY, False), bufs[2])
    y2 = Ring("layer", ny, 1, own_sum(qz), bufs[3])

    def multiply(piece):
        cols = pl.ds(pl.multiple_of(piece * PIECE, PIECE), PIECE)
        block = im[:, cols]
        tall = 512

        def body(r, carry):
            rows = abuf[pl.ds(r * (tall // CHUNK), tall // CHUNK)].reshape(tall, depth)
            product = jnp.dot(rows, block, preferred_element_type=jnp.float32)
            at = pl.ds(pl.multiple_of(r * tall, tall), tall)
            part[piece, 0, at, :] = product[:, :LANES]
            part[piece, 1, at, :] = product[:, LANES:]
            return carry

        lax.fori_loop(0, ny * nz * CHUNK // tall, body, 0)

    def store_sum(ref):
        def store(p, g, h, value):
            ref[p, h, pl.ds(g * CHUNK if isinstance(g, int) else pl.multiple_of(g * CHUNK, CHUNK), CHUNK), :] = value
        return store

    def store_out(base):
        def store(p, g, h, value):
            out[:, pl.ds(pl.multiple_of((base + p) * PIECE + h * LANES, LANES), LANES)] = value
        return store

    def y_start(p):
        multiply(p)
        y1.send(p, 0)

    def y_turn(p):
        y1.final(p, store_sum(qy))
        z2.send(p, 0)

    def z_start(p):
        multiply(NY + p)
        z1.send(p, 0)

    def z_turn(p):
        z1.final(p, store_sum(qz))
        y2.send(p, 0)

    y_stages = [y_start, lambda p: y1.send(p, 1), y_turn] + [functools.partial(lambda t, p: z2.send(p, t), t) for t in (1, 2, 3)]
    y_stages += [lambda p: z2.final(p, store_out(0))]
    z_stages = [z_start] + [functools.partial(lambda t, p: z1.send(p, t), t) for t in (1, 2, 3)]
    z_stages += [z_turn, lambda p: y2.send(p, 1), lambda p: y2.final(p, store_out(NY))]

    def tick(k, carry):
        for s in range(len(y_stages)):
            @pl.when((k >= s) & (k - s < NY))
            def _(s=s):
                y_stages[s](k - s)

            @pl.when((k >= s) & (k - s < n_z))
            def _(s=s):
                z_stages[s](k - s)
        return carry

    lax.fori_loop(0, NY + len(y_stages) - 1, tick, 0)

    for j in range(per_core):
        @pl.when(c * per_core + j != z)
        def _(j=j):
            along_z(j).wait_send()

    @pl.when(active)
    def _():
        for g in range(groups):
            for k in near:
                along_x(g, k).wait_send()
            for k in range(nx):
                xs = lax.rem(x + k, nx)

                @pl.when(xs != y)
                def _(g=g, k=k, xs=xs):
                    along_y(g, k, xs).wait_send()
            for ys in range(ny):
                across(g, ys).wait_send()

    y1.drain(NY)
    z2.drain(NY)
    z1.drain(n_z)
    y2.drain(n_z)


def solution(mesh):
    ny, nz, nx = mesh.shape["layer"], mesh.shape["perm"], mesh.shape["owner"] // 2

    def local(amplitudes, integrals, contract_irrep, output_irrep, occ_energy, virt_energy):
        rows = amplitudes.shape[0]
        depth, width = integrals.shape
        pieces = width // PIECE
        n_z = pieces - NY
        groups = nz // 2
        dma = pltpu.SemaphoreType.DMA
        rings = []
        for n, count, size in ((ny, NY, nz), (nz, NY, 1), (nz, n_z, ny), (ny, n_z, 1)):
            rings += [pltpu.VMEM((count, n // 2, 2, 2, size * CHUNK, LANES), jnp.int16)] * 2
            rings += [pltpu.VMEM((count, n // 2, 2, size, LANES), jnp.float32)] * 2
            rings += [dma((4, count, n // 2, 2))]
        asems = (
            dma((nz // 2,)), dma((nz,)),
            dma((groups, nx)), dma((groups, nx)),
            dma((groups, nx)), dma((groups, ny)),
            dma((groups, ny)), dma((groups, ny)),
            dma((depth // BW,)),
        )
        ladder = pl.pallas_call(
            functools.partial(kernel, ny, nz, nx),
            out_shape=jax.ShapeDtypeStruct((rows, width), jnp.float32),
            in_specs=[pl.BlockSpec(memory_space=pltpu.SMEM)] * 2
            + [pl.BlockSpec(memory_space=pltpu.VMEM), pl.BlockSpec(memory_space=pl.ANY)],
            out_specs=pl.BlockSpec(memory_space=pltpu.VMEM),
            scratch_shapes=[
                pltpu.VMEM((2 * ny * nz, rows, depth), jnp.bfloat16),
                pltpu.VMEM((depth, width), jnp.bfloat16),
                pltpu.VMEM((pieces, 2, ny * nz * CHUNK, LANES), jnp.float32),
                pltpu.VMEM((NY, 2, nz * CHUNK, LANES), jnp.float32),
                pltpu.VMEM((n_z, 2, ny * CHUNK, LANES), jnp.float32),
                asems,
            ] + rings,
            compiler_params=pltpu.CompilerParams(
                collective_id=0, has_side_effects=True, vmem_limit_bytes=56 * 2**20
            ),
            cost_estimate=pl.CostEstimate(
                flops=2 * ny * nz * rows * depth * width, bytes_accessed=2 * depth * width, transcendentals=0
            ),
        )(contract_irrep, output_irrep, amplitudes, integrals)
        return ladder / (virt_energy[None, :] - occ_energy[:, None])

    return jax.shard_map(
        local,
        mesh=mesh,
        in_specs=(
            P(("layer", "perm"), "owner"),
            P(("layer", "perm"), "owner"),
            P(),
            P(),
            P(("layer", "perm")),
            P("owner"),
        ),
        out_specs=P(("layer", "perm"), "owner"),
        check_vma=False,
    )
```

time: 357 us -> 82.9 us (0.23)
  waiting for transfers between devices: 292 us -> 0 us
  Pallas kernels: 0 us -> 80.1 us
  other arithmetic: 16.9 us -> 1.76 us
  local copies, waits for them, and re-layouts: 13.9 us -> 0.01 us
  between operations: 13.5 us -> 0.03 us
  starting transfers between devices: 10.2 us -> 0 us
  matrix products: 9.64 us -> 0 us
    reduce_scatter x1 -> x0, waiting for transfers between devices: 227 us -> none  [local(): lax.psum_scatter(jnp.dot(ordered, sector, preferred_element_type=jnp.floa...]
    pallas_call x0 -> x1, Pallas kernels: none -> 80.1 us  [local(): pl.pallas_call(functools.partial(kernel, ny, nz, nx), out_shape=jax.Shape...]
    all_gather x1 -> x0, waiting for transfers between devices: 32.5 us -> none  [local(): gathered = lax.all_gather(amplitudes, 'owner', axis=1, tiled=True)]
    all_to_all x1 -> x0, waiting for transfers between devices: 31.1 us -> none  [local(): lax.all_to_all(gathered, ('layer', 'perm'), split_axis=1, concat_axis=0,...]
    all_to_all x1 -> x0, starting transfers between devices: 10.2 us -> none  [local(): lax.all_to_all(gathered, ('layer', 'perm'), split_axis=1, concat_axis=0,...]
    dot_general x1 -> x0, matrix products: 9.64 us -> none  [local(): jnp.dot(ordered, sector, preferred_element_type=jnp.float32)]
    unnamed x9 -> x4, local copies, waits for them, and re-layouts: 9.15 us -> 0.01 us
    gather x4 -> x0, other arithmetic: 8.81 us -> none  [the longest x2 4.52 us: local(): jnp.repeat(lax.dynamic_slice_in_dim(output_irrep, outer_offset, outer_blo...]
  transfers between devices with their start and end apart: 3 -> 0, of which waited for: 3 -> 0; matrix products, arithmetic and copies ran while one was open for 5% -> 0% of each run, Pallas kernels for 0% -> 0%
where the time goes in v1:
time: 82.9 us; the launch traced here: 81.9 us
  Pallas kernels  80.1 us (97%)
  other arithmetic  1.76 us (2%)
    pallas_call x1, Pallas kernels, local(): pl.pallas_call(functools.partial(kernel, ny, nz, nx), out_shape=jax.Shape...  80.1 us
    div x1, other arithmetic, local(): return ladder / (virt_energy[None, :] - occ_energy[:, None])  1.76 us

profile of v1, /device:TPU:8, one launch (start us, length us, event | category | flops | bytes accessed | tf_op | source)
XLA Modules:
  0.0 81.9 jit_solution(13747593715788150518)
XLA Ops:
  0.0 0.0 copy-start
  0.0 0.0 copy-start.1
  0.0 80.1 %shard_map.64 = f32[32,2048]{1,0:T(8,128)} custom-call(s32[256]{0:T(256)} %cirr.1, s32[128]{0:T(128)} %oirr.1, bf16[32,4096]{1,0:T(8,128)(2,1)} %amp.1, bf16[1024,2048]{1,0:T(8,128)(2,1)} %integ.1), custom_call_target="tpu_custom_call" | custom-call | flops 4294967296 | bytes 4194304 | tf_op jit(solution)/shard_map/pallas_call | solution.py:395
  80.1 0.0 copy-done
  80.1 0.0 copy-done.1
  80.1 1.8 %subtract_divide_fusion = f32[32,2048]{1,0:T(8,128)} fusion(f32[32,2048]{1,0:T(8,128)} %shard_map.64, f32[32]{0:T(128)S(1)} %copy-done.1, f32[2048]{0:T(1024)S(1)} %copy-done), kind=kLoop, calls=%fused_computation | loop fusion | flops 131072 | bytes 532608 | tf_op jit(solution)/shard_map/div | solution.py:416
Async XLA Ops:
  0.0 80.1 %copy-start = (f32[2048]{0:T(1024)S(1)}, f32[2048]{0:T(1024)}, u32[]{:S(2)}) copy-start(f32[2048]{0:T(1024)} %param.11) | copy-start | bytes 24580
  0.0 80.1 %copy-start.1 = (f32[32]{0:T(128)S(1)}, f32[32]{0:T(128)}, u32[]{:S(2)}) copy-start(f32[32]{0:T(128)} %param.10) | copy-start | bytes 388

commit v2 on v0

v2 whole, which is shorter than its diff:
```python
import functools

import jax
import jax.numpy as jnp
from jax import lax
from jax.experimental import pallas as pl
from jax.experimental.pallas import tpu as pltpu
from jax.sharding import PartitionSpec as P

BW = 128
LANES = 128
CHUNK = 32
PIECE = 256
TOP = 32767.0
MESH = pl.DeviceIdType.MESH

Y_GROUPS = ((0, 3), (3, 2))
Z_GROUPS = ((0, 1), (1, 1), (2, 1))
Z_ALL = ((0, 3),)
NY, NZ = 5, 3


class Ring:
    def __init__(self, axis, n, slots, groups, own, bufs):
        self.axis, self.n, self.slots, self.groups, self.own = axis, n, slots, groups, own
        self.sq, self.rq, self.ss, self.rs, self.sems = bufs
        self.me = lax.axis_index(axis)

    def copies(self, v, t, d, g):
        where = {self.axis: lax.rem(self.me + (1 if d == 0 else self.n - 1), self.n)}
        first, count = self.groups[g]
        rows, pieces = pl.ds(0, self.slots[v]), pl.ds(first, count)
        at = (v, t, d, rows, pieces, d) if t == 0 else (v, t, d, rows, pieces)
        scales = (v, t, d, rows, pieces)
        return [
            pltpu.make_async_remote_copy(
                src_ref=self.sq.at[at],
                dst_ref=self.rq.at[at],
                send_sem=self.sems.at[0, v, t, d, g],
                recv_sem=self.sems.at[1, v, t, d, g],
                device_id=where,
                device_id_type=MESH,
            ),
            pltpu.make_async_remote_copy(
                src_ref=self.ss.at[scales],
                dst_ref=self.rs.at[scales],
                send_sem=self.sems.at[2, v, t, d, g],
                recv_sem=self.sems.at[3, v, t, d, g],
                device_id=where,
                device_id_type=MESH,
            ),
        ]

    def each(self, v, g, body):
        first, count = self.groups[g]
        total = self.slots[v] * count

        def step(k, carry):
            body(k // count, first + lax.rem(k, count))
            return carry

        lax.fori_loop(0, total, step, 0, unroll=2 if total % 2 == 0 else 1)

    def decode(self, v, t, d, s, p, h):
        return self.rq[v, t, d, s, p, h].astype(jnp.int32).astype(jnp.float32) * self.rs[v, t, d, s, p]

    def wait(self, v, t, d, g):
        for copy in self.copies(v, t, d, g):
            copy.wait_recv()

    def send(self, v, t, g):
        for d in range(2):
            if t > 0:
                self.wait(v, t - 1, d, g)

            def body(s, p, d=d):
                halves = (d,) if t == 0 else (0, 1)
                values = []
                for h in halves:
                    value = self.own(v, t, d, s, p, h)
                    if t > 1 or (t == 1 and h == d):
                        value = value + self.decode(v, t - 1, d, s, p, h)
                    values.append(value)
                most = jnp.max(functools.reduce(jnp.maximum, [jnp.abs(u) for u in values]), axis=0, keepdims=True)
                scale = jnp.maximum(most, 1e-30) * (1.0 / TOP)
                factor = 1.0 / scale
                self.ss[v, t, d, s, p] = scale
                for h, value in zip(halves, values):
                    self.sq[v, t, d, s, p, h] = jnp.round(value * factor).astype(jnp.int32).astype(jnp.int16)

            self.each(v, g, body)
            for copy in self.copies(v, t, d, g):
                copy.start()

    def final(self, v, g, store):
        last = self.n // 2 - 1
        for d in range(2):
            self.wait(v, last, d, g)

        def body(s, p):
            for h in range(2):
                total = self.own(v, None, None, s, p, h) + self.decode(v, last, 0, s, p, h)
                store(s, p, h, total + self.decode(v, last, 1, s, p, h))

        self.each(v, g, body)

    def drain(self):
        for v in range(len(self.slots)):
            for t in range(self.n // 2):
                for d in range(2):
                    for g in range(len(self.groups)):
                        for copy in self.copies(v, t, d, g):
                            copy.wait_send()


def kernel(ny, nz, nx, cirr, oirr, amp, integ, out, abuf, im, part, qy, qz, asems, *ring_bufs):
    y, z, o = lax.axis_index("layer"), lax.axis_index("perm"), lax.axis_index("owner")
    x, c = o // 2, lax.rem(o, 2)
    depth, width = im.shape
    half = nz // 2
    a_send, a_recv, x_send, x_recv, b_send, b_recv, i_sem = asems
    active = c == z // half
    sibling = {"owner": o + 1 - 2 * c}

    def row_of(column, zs, at_z):
        return lax.rem(column + 4 * nx - zs - at_z, nx)

    barrier = pltpu.get_barrier_semaphore()

    def greet(where):
        pl.semaphore_signal(barrier, inc=1, device_id=where, device_id_type=MESH)

    for k in (1, nz - 1):
        greet({"perm": lax.rem(z + k, nz)})
    for k in (1, ny - 1):
        greet({"layer": lax.rem(y + k, ny)})
    for k in range(1, nx):
        greet({"owner": lax.rem(o + 2 * k, 2 * nx)})
    greet(sibling)
    for zs in range(nz):
        ys = row_of(x, zs, z)

        @pl.when(active & jnp.logical_not((x == y) & (ys == y) & (z == zs)))
        def _(zs=zs, ys=ys):
            greet({"owner": 2 * y + c, "layer": ys, "perm": jnp.int32(zs)})

    load = [
        pltpu.make_async_copy(integ.at[pl.ds(k * BW, BW)], im.at[pl.ds(k * BW, BW)], i_sem.at[k])
        for k in range(depth // BW)
    ]
    for copy in load:
        copy.start()

    def block(k):
        j = lax.rem(z + jnp.where(active, (2, 1, 3, 0)[k], (0, 1, 3, 2)[k]), half)
        to_z = half * c + j
        column = lax.rem(y + z + to_z, nx)
        mine = (column == x) & (x == y) & (to_z == z)
        source = amp.at[:, pl.ds(pl.multiple_of(j * depth, depth), depth)]
        remote = pltpu.make_async_remote_copy(
            src_ref=source,
            dst_ref=abuf.at[z, y],
            send_sem=a_send.at[k],
            recv_sem=a_recv.at[z],
            device_id={"owner": 2 * column + c, "layer": x, "perm": to_z},
            device_id_type=MESH,
        )
        return mine, remote, pltpu.make_async_copy(source, abuf.at[z, y], a_recv.at[z])

    keeps = active & (x == y) & (lax.rem(y + 2 * z, nx) == x)
    pl.semaphore_wait(barrier, nx + 4 + half - keeps.astype(jnp.int32))
    for k in range(half):
        mine, remote, here = block(k)

        @pl.when(jnp.logical_not(mine))
        def _(remote=remote):
            remote.start()

        @pl.when(mine)
        def _(here=here):
            here.start()

    outer = width // BW
    inner_base = (y * nz + z) * (depth // BW)
    outer_base = o * outer
    for copy in load:
        copy.wait()

    def mask_rows(k, carry):
        row_irrep = cirr[inner_base + k]
        rows = pl.ds(pl.multiple_of(k * BW, BW), BW)
        for b in range(outer):
            cols = pl.ds(b * BW, BW)
            values = im[rows, cols]
            im[rows, cols] = jnp.where(row_irrep == oirr[outer_base + b], values, jnp.zeros_like(values))
        return carry

    lax.fori_loop(0, depth // BW, mask_rows, 0)

    def places(u):
        if u == 0:
            return [lax.rem(z + half, nz)]
        if u == half:
            return [z]
        return [lax.rem(z + half - u, nz), lax.rem(z + half + u, nz)]

    def along_x(zs, k):
        ys = row_of(x, zs, z)
        return pltpu.make_async_remote_copy(
            src_ref=abuf.at[zs, ys],
            dst_ref=abuf.at[zs, ys],
            send_sem=x_send.at[zs, k],
            recv_sem=x_recv.at[zs, k],
            device_id={"owner": lax.rem(o + 2 * k, 2 * nx)},
            device_id_type=MESH,
        )

    def across(zs):
        return pltpu.make_async_remote_copy(
            src_ref=abuf.at[zs],
            dst_ref=abuf.at[zs],
            send_sem=b_send.at[zs],
            recv_sem=b_recv.at[zs],
            device_id=sibling,
            device_id_type=MESH,
        )

    def spread(u):
        if u > half:
            return

        @pl.when(active)
        def _():
            for zs in places(u):
                ys = row_of(x, zs, z)
                pltpu.make_async_copy(abuf.at[zs, ys], abuf.at[zs, ys], a_recv.at[zs]).wait()
                for k in range(1, nx):
                    along_x(zs, k).start()

    def collect(u):
        if u > half:
            return

        @pl.when(active)
        def _():
            for zs in places(u):
                for k in range(1, nx):
                    ys = row_of(lax.rem(x + nx - k, nx), zs, z)
                    pltpu.make_async_copy(abuf.at[zs, ys], abuf.at[zs, ys], x_recv.at[zs, k]).wait()
                across(zs).start()

    def arrive(u):
        @pl.when(jnp.logical_not(active))
        def _():
            for zs in places(u):
                across(zs).wait_recv()

    tall = ny * CHUNK

    def multiply(u, first, count):
        def body(k, carry):
            piece = first + k
            right = im[:, pl.ds(pl.multiple_of(piece * PIECE, PIECE), PIECE)]
            left = [abuf[zs].reshape(tall, depth) for zs in places(u)]
            product = jnp.dot(jnp.concatenate(left, axis=0), right, preferred_element_type=jnp.float32)
            for k, zs in enumerate(places(u)):
                at = pl.ds(pl.multiple_of(zs * tall, tall), tall)
                part[piece, 0, at, :] = product[k * tall: (k + 1) * tall, :LANES]
                part[piece, 1, at, :] = product[k * tall: (k + 1) * tall, LANES:]
            return carry

        lax.fori_loop(0, count, body, 0)

    def toward(me, n, t, d):
        if t is None:
            return me
        return lax.rem(me + (n // 2 - t if d == 0 else n // 2 + t), n)

    def rows_at(piece, h, at_z, at_y):
        return part[piece, h, pl.ds(pl.multiple_of((at_z * ny + at_y) * CHUNK, CHUNK), CHUNK), :]

    def y1_own(v, t, d, s, p, h):
        where = places(v)
        at_z = where[0] if len(where) == 1 else jnp.where(s == 0, where[0], where[1])
        return rows_at(p, h, at_z, toward(y, ny, t, d))

    def z1_own(v, t, d, s, p, h):
        return rows_at(NY + p, h, toward(z, nz, t, d), s)

    def z2_own(v, t, d, s, p, h):
        return qy[nz - 1 if t is None else 0 if t == 0 else 2 * t - 1 + d, p, h]

    def y2_own(v, t, d, s, p, h):
        return qz[toward(y, ny, t, d), p, h]

    bufs = [ring_bufs[5 * k: 5 * k + 5] for k in range(4)]
    y1 = Ring("layer", ny, [len(places(u)) for u in range(half + 1)], Y_GROUPS, y1_own, bufs[0])
    z2 = Ring("perm", nz, [1], Y_GROUPS, z2_own, bufs[1])
    z1 = Ring("perm", nz, [ny], Z_GROUPS, z1_own, bufs[2])
    y2 = Ring("layer", ny, [1], Z_ALL, y2_own, bufs[3])

    def keep_y(u):
        def store(s, p, h, value):
            qy[max(2 * u - 1, 0) + s, p, h] = value
        return store

    def keep_z(s, p, h, value):
        qz[s, p, h] = value

    def write(base):
        def store(s, p, h, value):
            out[:, pl.ds(pl.multiple_of((base + p) * PIECE + h * LANES, LANES), LANES)] = value
        return store

    spread(0)
    spread(1)
    collect(0)
    for i in range(half + 3):
        if i <= half:
            spread(i + 2)
            arrive(i)
            for g, (first, count) in enumerate(Y_GROUPS):
                multiply(i, first, count)
                y1.send(i, 0, g)
        if 1 <= i <= half + 1:
            for g in range(len(Y_GROUPS)):
                y1.send(i - 1, 1, g)
        if i <= half:
            for g, (first, count) in enumerate(Z_GROUPS):
                multiply(i, NY + first, count)
                if i < half:
                    z1.send(0, i, g)
                else:
                    z1.final(0, g, keep_z)
            collect(i + 1)
        if i == half:
            y2.send(0, 0, 0)
        if i == half + 1:
            y2.send(0, 1, 0)
        if i == half + 2:
            y2.final(0, 0, write(NY))
        if i >= 2:
            u = i - 2
            for g in range(len(Y_GROUPS)):
                y1.final(u, g, keep_y(u))
                if u < half:
                    z2.send(0, u, g)
                else:
                    z2.final(0, g, write(0))

    for k in range(half):
        mine, remote, here = block(k)

        @pl.when(jnp.logical_not(mine))
        def _(remote=remote):
            remote.wait_send()

    @pl.when(active)
    def _():
        for zs in range(nz):
            for k in range(1, nx):
                along_x(zs, k).wait_send()
            across(zs).wait_send()

    for ring in (y1, z2, z1, y2):
        ring.drain()


def solution(mesh):
    ny, nz, nx = mesh.shape["layer"], mesh.shape["perm"], mesh.shape["owner"] // 2

    def local(amplitudes, integrals, contract_irrep, output_irrep, occ_energy, virt_energy):
        rows = amplitudes.shape[0]
        depth, width = integrals.shape
        dma = pltpu.SemaphoreType.DMA
        rings = []
        for n, turns, slots, pieces, groups in (
            (ny, nz // 2 + 1, 2, NY, len(Y_GROUPS)),
            (nz, 1, 1, NY, len(Y_GROUPS)),
            (nz, 1, ny, NZ, len(Z_GROUPS)),
            (ny, 1, 1, NZ, len(Z_ALL)),
        ):
            rings += [pltpu.VMEM((turns, n // 2, 2, slots, pieces, 2, CHUNK, LANES), jnp.int16)] * 2
            rings += [pltpu.VMEM((turns, n // 2, 2, slots, pieces, 1, LANES), jnp.float32)] * 2
            rings += [dma((4, turns, n // 2, 2, groups))]
        asems = (
            dma((nz // 2,)), dma((nz,)),
            dma((nz, nx)), dma((nz, nx)),
            dma((nz,)), dma((nz,)),
            dma((depth // BW,)),
        )
        ladder = pl.pallas_call(
            functools.partial(kernel, ny, nz, nx),
            out_shape=jax.ShapeDtypeStruct((rows, width), jnp.float32),
            in_specs=[pl.BlockSpec(memory_space=pltpu.SMEM)] * 2 + [pl.BlockSpec(memory_space=pl.ANY)] * 2,
            out_specs=pl.BlockSpec(memory_space=pltpu.VMEM),
            scratch_shapes=[
                pltpu.VMEM((nz, ny, rows, depth), jnp.bfloat16),
                pltpu.VMEM((depth, width), jnp.bfloat16),
                pltpu.VMEM((NY + NZ, 2, ny * nz * CHUNK, LANES), jnp.float32),
                pltpu.VMEM((nz, NY, 2, CHUNK, LANES), jnp.float32),
                pltpu.VMEM((ny, NZ, 2, CHUNK, LANES), jnp.float32),
                asems,
            ] + rings,
            compiler_params=pltpu.CompilerParams(
                collective_id=0, has_side_effects=True, vmem_limit_bytes=56 * 2**20
            ),
            cost_estimate=pl.CostEstimate(
                flops=2 * ny * nz * rows * depth * width, bytes_accessed=2 * depth * width, transcendentals=0
            ),
        )(contract_irrep, output_irrep, amplitudes, integrals)
        return ladder / (virt_energy[None, :] - occ_energy[:, None])

    return jax.shard_map(
        local,
        mesh=mesh,
        in_specs=(
            P(("layer", "perm"), "owner"),
            P(("layer", "perm"), "owner"),
            P(),
            P(),
            P(("layer", "perm")),
            P("owner"),
        ),
        out_specs=P(("layer", "perm"), "owner"),
        check_vma=False,
    )
```

time: 357 us -> 64.2 us (0.18)
  the two profiles are of different devices: /device:TPU:8 before, /device:TPU:1 now
where the time goes in v2:
time: 64.2 us; the launch traced here: 64 us
  Pallas kernels  62.2 us (97%)
  other arithmetic  1.76 us (3%)
    pallas_call x1, Pallas kernels, local(): pl.pallas_call(functools.partial(kernel, ny, nz, nx), out_shape=jax.Shape...  62.2 us
    div x1, other arithmetic, local(): return ladder / (virt_energy[None, :] - occ_energy[:, None])  1.76 us

profile of v2, /device:TPU:1, one launch (start us, length us, event | category | flops | bytes accessed | tf_op | source)
XLA Modules:
  0.0 64.0 jit_solution(9271299638044535701)
XLA Ops:
  0.0 0.0 copy-start
  0.0 0.0 copy-start.1
  0.0 62.2 %shard_map.64 = f32[32,2048]{1,0:T(8,128)} custom-call(s32[256]{0:T(256)} %cirr.1, s32[128]{0:T(128)} %oirr.1, bf16[32,4096]{1,0:T(8,128)(2,1)} %amp.1, bf16[1024,2048]{1,0:T(8,128)(2,1)} %integ.1), custom_call_target="tpu_custom_call" | custom-call | flops 4294967296 | bytes 4194304 | tf_op jit(solution)/shard_map/pallas_call | solution.py:392
  62.2 0.0 copy-done
  62.2 0.0 copy-done.1
  62.2 1.8 %subtract_divide_fusion = f32[32,2048]{1,0:T(8,128)} fusion(f32[32,2048]{1,0:T(8,128)} %shard_map.64, f32[32]{0:T(128)S(1)} %copy-done.1, f32[2048]{0:T(1024)S(1)} %copy-done), kind=kLoop, calls=%fused_computation | loop fusion | flops 131072 | bytes 532608 | tf_op jit(solution)/shard_map/div | solution.py:412
Async XLA Ops:
  0.0 62.2 %copy-start = (f32[2048]{0:T(1024)S(1)}, f32[2048]{0:T(1024)}, u32[]{:S(2)}) copy-start(f32[2048]{0:T(1024)} %param.11) | copy-start | bytes 24580
  0.0 62.2 %copy-start.1 = (f32[32]{0:T(128)S(1)}, f32[32]{0:T(128)}, u32[]{:S(2)}) copy-start(f32[32]{0:T(128)} %param.10) | copy-start | bytes 388

commit v3 on v2

--- a/solution.py
+++ b/solution.py
@@ -25,6 +25,7 @@
         self.axis, self.n, self.slots, self.groups, self.own = axis, n, slots, groups, own
         self.sq, self.rq, self.ss, self.rs, self.sems = bufs
         self.me = lax.axis_index(axis)
+        self.started = []
 
     def copies(self, v, t, d, g):
         where = {self.axis: lax.rem(self.me + (1 if d == 0 else self.n - 1), self.n)}
@@ -91,6 +92,7 @@
             self.each(v, g, body)
             for copy in self.copies(v, t, d, g):
                 copy.start()
+        self.started.append((v, t, g))
 
     def final(self, v, g, store):
         last = self.n // 2 - 1
@@ -104,13 +106,13 @@
 
         self.each(v, g, body)
 
-    def drain(self):
-        for v in range(len(self.slots)):
-            for t in range(self.n // 2):
-                for d in range(2):
-                    for g in range(len(self.groups)):
-                        for copy in self.copies(v, t, d, g):
-                            copy.wait_send()
+    def drain(self, keep=0):
+        count = max(len(self.started) - keep, 0)
+        for v, t, g in self.started[:count]:
+            for d in range(2):
+                for copy in self.copies(v, t, d, g):
+                    copy.wait_send()
+        self.started = self.started[count:]
 
 
 def kernel(ny, nz, nx, cirr, oirr, amp, integ, out, abuf, im, part, qy, qz, asems, *ring_bufs):
@@ -130,6 +132,13 @@
     def greet(where):
         pl.semaphore_signal(barrier, inc=1, device_id=where, device_id_type=MESH)
 
+    for zs in range(nz):
+        ys = row_of(x, zs, z)
+
+        @pl.when(active & jnp.logical_not((x == y) & (ys == y) & (z == zs)))
+        def _(zs=zs, ys=ys):
+            greet({"owner": 2 * y + c, "layer": ys, "perm": jnp.int32(zs)})
+
     for k in (1, nz - 1):
         greet({"perm": lax.rem(z + k, nz)})
     for k in (1, ny - 1):
@@ -137,12 +146,6 @@
     for k in range(1, nx):
         greet({"owner": lax.rem(o + 2 * k, 2 * nx)})
     greet(sibling)
-    for zs in range(nz):
-        ys = row_of(x, zs, z)
-
-        @pl.when(active & jnp.logical_not((x == y) & (ys == y) & (z == zs)))
-        def _(zs=zs, ys=ys):
-            greet({"owner": 2 * y + c, "layer": ys, "perm": jnp.int32(zs)})
 
     load = [
         pltpu.make_async_copy(integ.at[pl.ds(k * BW, BW)], im.at[pl.ds(k * BW, BW)], i_sem.at[k])
@@ -151,8 +154,15 @@
     for copy in load:
         copy.start()
 
+    orders = (((0, 1, 2, 3), (1, 0, 2, 3), (2, 1, 3, 0), (3, 2, 1, 0)), ((3, 2, 1, 0), (3, 0, 2, 1), (0, 1, 3, 2), (0, 1, 2, 3)))
+
     def block(k):
-        j = lax.rem(z + jnp.where(active, (2, 1, 3, 0)[k], (0, 1, 3, 2)[k]), half)
+        turn = lax.rem(z, half)
+        far, near = [
+            functools.reduce(lambda rest, r: jnp.where(turn == r, order[r][k], rest), range(1, half), order[0][k])
+            for order in orders
+        ]
+        j = jnp.where(active, near, far)
         to_z = half * c + j
         column = lax.rem(y + z + to_z, nx)
         mine = (column == x) & (x == y) & (to_z == z)
@@ -312,16 +322,46 @@
             out[:, pl.ds(pl.multiple_of((base + p) * PIECE + h * LANES, LANES), LANES)] = value
         return store
 
+    def brought():
+        for k in range(half):
+            mine, remote, here = block(k)
+
+            @pl.when(jnp.logical_not(mine))
+            def _(remote=remote):
+                remote.wait_send()
+
+    def spread_left(u):
+        if u > half:
+            return
+
+        @pl.when(active)
+        def _():
+            for zs in places(u):
+                for k in range(1, nx):
+                    along_x(zs, k).wait_send()
+                across(zs).wait_send()
+
     spread(0)
     spread(1)
+    spread(2)
+    spread(3)
+    spread(4)
     collect(0)
     for i in range(half + 3):
         if i <= half:
-            spread(i + 2)
+            spread(i + 5)
+            collect(i + 1)
             arrive(i)
             for g, (first, count) in enumerate(Y_GROUPS):
                 multiply(i, first, count)
                 y1.send(i, 0, g)
+        if i == 1:
+            brought()
+        if i >= 1:
+            spread_left(i - 1)
+            y1.drain(2 * len(Y_GROUPS))
+            z2.drain(len(Y_GROUPS))
+            z1.drain(len(Z_GROUPS))
         if 1 <= i <= half + 1:
             for g in range(len(Y_GROUPS)):
                 y1.send(i - 1, 1, g)
@@ -332,7 +372,6 @@
                     z1.send(0, i, g)
                 else:
                     z1.final(0, g, keep_z)
-            collect(i + 1)
         if i == half:
             y2.send(0, 0, 0)
         if i == half + 1:
@@ -347,20 +386,6 @@
                     z2.send(0, u, g)
                 else:
                     z2.final(0, g, write(0))
-
-    for k in range(half):
-        mine, remote, here = block(k)
-
-        @pl.when(jnp.logical_not(mine))
-        def _(remote=remote):
-            remote.wait_send()
-
-    @pl.when(active)
-    def _():
-        for zs in range(nz):
-            for k in range(1, nx):
-                along_x(zs, k).wait_send()
-            across(zs).wait_send()
 
     for ring in (y1, z2, z1, y2):
         ring.drain()

time: 64.2 us -> 63.5 us (0.989)
  the two profiles are of different devices: /device:TPU:1 before, /device:TPU:8 now
where the time goes in v3:
time: 63.5 us; the launch traced here: 63.4 us
  Pallas kernels  61.6 us (97%)
  other arithmetic  1.76 us (3%)
    pallas_call x1, Pallas kernels, local(): pl.pallas_call(functools.partial(kernel, ny, nz, nx), out_shape=jax.Shape...  61.6 us
    div x1, other arithmetic, local(): return ladder / (virt_energy[None, :] - occ_energy[:, None])  1.76 us

profile of v3, /device:TPU:8, one launch (start us, length us, event | category | flops | bytes accessed | tf_op | source)
XLA Modules:
  0.0 63.4 jit_solution(13506942027163483188)
XLA Ops:
  0.0 0.0 copy-start
  0.0 0.0 copy-start.1
  0.0 61.6 %shard_map.64 = f32[32,2048]{1,0:T(8,128)} custom-call(s32[256]{0:T(256)} %cirr.1, s32[128]{0:T(128)} %oirr.1, bf16[32,4096]{1,0:T(8,128)(2,1)} %amp.1, bf16[1024,2048]{1,0:T(8,128)(2,1)} %integ.1), custom_call_target="tpu_custom_call" | custom-call | flops 4294967296 | bytes 4194304 | tf_op jit(solution)/shard_map/pallas_call | solution.py:417
  61.6 0.0 copy-done
  61.6 0.0 copy-done.1
  61.6 1.8 %subtract_divide_fusion = f32[32,2048]{1,0:T(8,128)} fusion(f32[32,2048]{1,0:T(8,128)} %shard_map.64, f32[32]{0:T(128)S(1)} %copy-done.1, f32[2048]{0:T(1024)S(1)} %copy-done), kind=kLoop, calls=%fused_computation | loop fusion | flops 131072 | bytes 532608 | tf_op jit(solution)/shard_map/div | solution.py:437
Async XLA Ops:
  0.0 61.6 %copy-start = (f32[2048]{0:T(1024)S(1)}, f32[2048]{0:T(1024)}, u32[]{:S(2)}) copy-start(f32[2048]{0:T(1024)} %param.11) | copy-start | bytes 24580
  0.0 61.6 %copy-start.1 = (f32[32]{0:T(128)S(1)}, f32[32]{0:T(128)}, u32[]{:S(2)}) copy-start(f32[32]{0:T(128)} %param.10) | copy-start | bytes 388

commit v4 on v3

--- a/solution.py
+++ b/solution.py
@@ -60,7 +60,7 @@
             body(k // count, first + lax.rem(k, count))
             return carry
 
-        lax.fori_loop(0, total, step, 0, unroll=2 if total % 2 == 0 else 1)
+        lax.fori_loop(0, total, step, 0, unroll=next(w for w in (4, 5, 3, 2, 1) if total % w == 0))
 
     def decode(self, v, t, d, s, p, h):
         return self.rq[v, t, d, s, p, h].astype(jnp.int32).astype(jnp.float32) * self.rs[v, t, d, s, p]
@@ -244,7 +244,7 @@
             for zs in places(u):
                 ys = row_of(x, zs, z)
                 pltpu.make_async_copy(abuf.at[zs, ys], abuf.at[zs, ys], a_recv.at[zs]).wait()
-                for k in range(1, nx):
+                for k in (2, 1, 3):
                     along_x(zs, k).start()
 
     def collect(u):
@@ -365,6 +365,14 @@
         if 1 <= i <= half + 1:
             for g in range(len(Y_GROUPS)):
                 y1.send(i - 1, 1, g)
+        if i >= 2:
+            u = i - 2
+            for g in range(len(Y_GROUPS)):
+                y1.final(u, g, keep_y(u))
+                if u < half:
+                    z2.send(0, u, g)
+                else:
+                    z2.final(0, g, write(0))
         if i <= half:
             for g, (first, count) in enumerate(Z_GROUPS):
                 multiply(i, NY + first, count)
@@ -378,14 +386,6 @@
             y2.send(0, 1, 0)
         if i == half + 2:
             y2.final(0, 0, write(NY))
-        if i >= 2:
-            u = i - 2
-            for g in range(len(Y_GROUPS)):
-                y1.final(u, g, keep_y(u))
-                if u < half:
-                    z2.send(0, u, g)
-                else:
-                    z2.final(0, g, write(0))
 
     for ring in (y1, z2, z1, y2):
         ring.drain()

time: 63.5 us -> 62.7 us (0.987)
  Pallas kernels: 61.6 us -> 60.8 us
    pallas_call x1, Pallas kernels: 61.6 us -> 60.8 us  [local(): pl.pallas_call(functools.partial(kernel, ny, nz, nx), out_shape=jax.Shape...]
where the time goes in v4:
time: 62.7 us; the launch traced here: 62.6 us
  Pallas kernels  60.8 us (97%)
  other arithmetic  1.76 us (3%)
    pallas_call x1, Pallas kernels, local(): pl.pallas_call(functools.partial(kernel, ny, nz, nx), out_shape=jax.Shape...  60.8 us
    div x1, other arithmetic, local(): return ladder / (virt_energy[None, :] - occ_energy[:, None])  1.76 us

profile of v4, /device:TPU:8, one launch (start us, length us, event | category | flops | bytes accessed | tf_op | source)
XLA Modules:
  0.0 62.6 jit_solution(12802447607073830850)
XLA Ops:
  0.0 0.0 copy-start
  0.0 0.0 copy-start.1
  0.0 60.8 %shard_map.64 = f32[32,2048]{1,0:T(8,128)} custom-call(s32[256]{0:T(256)} %cirr.1, s32[128]{0:T(128)} %oirr.1, bf16[32,4096]{1,0:T(8,128)(2,1)} %amp.1, bf16[1024,2048]{1,0:T(8,128)(2,1)} %integ.1), custom_call_target="tpu_custom_call" | custom-call | flops 4294967296 | bytes 4194304 | tf_op jit(solution)/shard_map/pallas_call | solution.py:417
  60.8 0.0 copy-done
  60.8 0.0 copy-done.1
  60.8 1.8 %subtract_divide_fusion = f32[32,2048]{1,0:T(8,128)} fusion(f32[32,2048]{1,0:T(8,128)} %shard_map.64, f32[32]{0:T(128)S(1)} %copy-done.1, f32[2048]{0:T(1024)S(1)} %copy-done), kind=kLoop, calls=%fused_computation | loop fusion | flops 131072 | bytes 532608 | tf_op jit(solution)/shard_map/div | solution.py:437
Async XLA Ops:
  0.0 60.8 %copy-start = (f32[2048]{0:T(1024)S(1)}, f32[2048]{0:T(1024)}, u32[]{:S(2)}) copy-start(f32[2048]{0:T(1024)} %param.11) | copy-start | bytes 24580
  0.0 60.8 %copy-start.1 = (f32[32]{0:T(128)S(1)}, f32[32]{0:T(128)}, u32[]{:S(2)}) copy-start(f32[32]{0:T(128)} %param.10) | copy-start | bytes 388

commit v5 on v4

--- a/solution.py
+++ b/solution.py
@@ -115,12 +115,12 @@
         self.started = self.started[count:]
 
 
-def kernel(ny, nz, nx, cirr, oirr, amp, integ, out, abuf, im, part, qy, qz, asems, *ring_bufs):
+def kernel(ny, nz, nx, cirr, oirr, amp, integ, out, held, abuf, im, part, qy, qz, asems, *ring_bufs):
     y, z, o = lax.axis_index("layer"), lax.axis_index("perm"), lax.axis_index("owner")
     x, c = o // 2, lax.rem(o, 2)
     depth, width = im.shape
     half = nz // 2
-    a_send, a_recv, x_send, x_recv, b_send, b_recv, i_sem = asems
+    a_send, a_recv, x_send, x_recv, b_send, b_recv, i_sem, h_sem = asems
     active = c == z // half
     sibling = {"owner": o + 1 - 2 * c}
 
@@ -147,6 +147,8 @@
         greet({"owner": lax.rem(o + 2 * k, 2 * nx)})
     greet(sibling)
 
+    stage = pltpu.make_async_copy(amp, held, h_sem.at[0])
+    stage.start()
     load = [
         pltpu.make_async_copy(integ.at[pl.ds(k * BW, BW)], im.at[pl.ds(k * BW, BW)], i_sem.at[k])
         for k in range(depth // BW)
@@ -166,7 +168,7 @@
         to_z = half * c + j
         column = lax.rem(y + z + to_z, nx)
         mine = (column == x) & (x == y) & (to_z == z)
-        source = amp.at[:, pl.ds(pl.multiple_of(j * depth, depth), depth)]
+        source = held.at[:, pl.ds(pl.multiple_of(j * depth, depth), depth)]
         remote = pltpu.make_async_remote_copy(
             src_ref=source,
             dst_ref=abuf.at[z, y],
@@ -178,6 +180,7 @@
         return mine, remote, pltpu.make_async_copy(source, abuf.at[z, y], a_recv.at[z])
 
     keeps = active & (x == y) & (lax.rem(y + 2 * z, nx) == x)
+    stage.wait()
     pl.semaphore_wait(barrier, nx + 4 + half - keeps.astype(jnp.int32))
     for k in range(half):
         mine, remote, here = block(k)
@@ -413,6 +416,7 @@
             dma((nz, nx)), dma((nz, nx)),
             dma((nz,)), dma((nz,)),
             dma((depth // BW,)),
+            dma((1,)),
         )
         ladder = pl.pallas_call(
             functools.partial(kernel, ny, nz, nx),
@@ -420,6 +424,7 @@
             in_specs=[pl.BlockSpec(memory_space=pltpu.SMEM)] * 2 + [pl.BlockSpec(memory_space=pl.ANY)] * 2,
             out_specs=pl.BlockSpec(memory_space=pltpu.VMEM),
             scratch_shapes=[
+                pltpu.VMEM(amplitudes.shape, jnp.bfloat16),
                 pltpu.VMEM((nz, ny, rows, depth), jnp.bfloat16),
                 pltpu.VMEM((depth, width), jnp.bfloat16),
                 pltpu.VMEM((NY + NZ, 2, ny * nz * CHUNK, LANES), jnp.float32),

time: 62.7 us -> 62.5 us (level)
  no operation moved by 1% of the time
where the time goes in v5:
time: 62.5 us; the launch traced here: 62.4 us
  Pallas kernels  60.6 us (97%)
  other arithmetic  1.76 us (3%)
    pallas_call x1, Pallas kernels, local(): pl.pallas_call(functools.partial(kernel, ny, nz, nx), out_shape=jax.Shape...  60.6 us
    div x1, other arithmetic, local(): return ladder / (virt_energy[None, :] - occ_energy[:, None])  1.76 us

profile of v5, /device:TPU:8, one launch (start us, length us, event | category | flops | bytes accessed | tf_op | source)
XLA Modules:
  0.0 62.4 jit_solution(12801349890931066109)
XLA Ops:
  0.0 0.0 copy-start
  0.0 0.0 copy-start.1
  0.0 60.6 %shard_map.64 = f32[32,2048]{1,0:T(8,128)} custom-call(s32[256]{0:T(256)} %cirr.1, s32[128]{0:T(128)} %oirr.1, bf16[32,4096]{1,0:T(8,128)(2,1)} %amp.1, bf16[1024,2048]{1,0:T(8,128)(2,1)} %integ.1), custom_call_target="tpu_custom_call" | custom-call | flops 4294967296 | bytes 4194304 | tf_op jit(solution)/shard_map/pallas_call | solution.py:421
  60.6 0.0 copy-done
  60.6 0.0 copy-done.1
  60.6 1.8 %subtract_divide_fusion = f32[32,2048]{1,0:T(8,128)} fusion(f32[32,2048]{1,0:T(8,128)} %shard_map.64, f32[32]{0:T(128)S(1)} %copy-done.1, f32[2048]{0:T(1024)S(1)} %copy-done), kind=kLoop, calls=%fused_computation | loop fusion | flops 131072 | bytes 532608 | tf_op jit(solution)/shard_map/div | solution.py:442
Async XLA Ops:
  0.0 60.6 %copy-start = (f32[2048]{0:T(1024)S(1)}, f32[2048]{0:T(1024)}, u32[]{:S(2)}) copy-start(f32[2048]{0:T(1024)} %param.11) | copy-start | bytes 24580
  0.0 60.6 %copy-start.1 = (f32[32]{0:T(128)S(1)}, f32[32]{0:T(128)}, u32[]{:S(2)}) copy-start(f32[32]{0:T(128)} %param.10) | copy-start | bytes 388
